TPU v7x, 32 devices: a whole 2x2x4 slice. The times are simulated.
32 devices in a mesh: dp: 4 (over y, x), space: 8 (over z, core).
Axes of the slice: x: 2, y: 2, z: 4, core: 2. Of those that a mesh axis runs over, the one named last changes fastest.
Arguments:
- features: bfloat16 [4, 128, 128, 256], P('dp', 'space'), may hold values from -6 to 6
- heights: float32 [4, 128, 128], P('dp', 'space'), may hold values from 0.02 to 2
- cotangent: bfloat16 [4, 128, 128, 256], P('dp', 'space'), may hold values from -6 to 6
- weight_first: bfloat16 [3, 3, 256, 256], replicated, may hold values from -0.125 to 0.125
- weight_second: bfloat16 [3, 3, 256, 256], replicated, may hold values from -0.125 to 0.125
- shade_embed: bfloat16 [256], replicated, may hold values from -4 to 4
Outputs:
- grad_features: bfloat16 [4, 128, 128, 256], P('dp', 'space')
- grad_first: float32 [3, 3, 256, 256], replicated
- grad_second: float32 [3, 3, 256, 256], replicated
- grad_embed: float32 [256], replicated
All inputs are finite; a program needn't handle non-finite values.
Results may differ from a plain program's by a relative error of at most 0.012.
Values may be sent and summed in bfloat16 or wider, within the bound.
A program may use at most 64 MiB of HBM per device.

v0:
```python
import math
import jax
import jax.numpy as jnp
from jax import lax
from jax.sharding import PartitionSpec as P


def prefix(part, axis, combine, identity):
    place = lax.axis_index(axis)
    gathered = lax.all_gather(part, axis)
    state = jnp.zeros_like(part) + jnp.asarray(identity, part.dtype)

    def one(hop, state):
        return combine(state, lax.dynamic_index_in_dim(gathered, hop, 0, False))

    return lax.fori_loop(0, place, one, state)


def padded_2(cells, sides, width):
    for axis, dim in sides:
        count = lax.axis_size(axis)
        ends = count - 1
        head = lax.slice_in_dim(cells, 0, width, axis=dim)
        tail = lax.slice_in_dim(cells, cells.shape[dim] - width, cells.shape[dim], axis=dim)
        cells = jnp.concatenate(
            [
                lax.ppermute(tail, axis, [(i, (i + 1) % count) for i in range(ends)]),
                cells,
                lax.ppermute(head, axis, [((i + 1) % count, i) for i in range(ends)]),
            ],
            axis=dim,
        )
    return cells


def convolve(padded, kernel):
    return lax.conv_general_dilated(
        padded,
        kernel,
        (1, 1),
        ((0, 0), (1, 1)),
        dimension_numbers=("NHWC", "HWIO", "NHWC"),
        preferred_element_type=jnp.float32,
    )


def reversed_kernel(kernel):
    return jnp.transpose(jnp.flip(kernel, (0, 1)), (0, 1, 3, 2))


def silu_slope(values):
    sigma = jax.nn.sigmoid(values)
    return sigma * (1.0 + values * (1.0 - sigma))


def kernel_grad(padded, gradient):
    channels = gradient.shape[-1]
    row_count = gradient.shape[1]
    col_count = gradient.shape[2]
    widened = jnp.pad(padded, ((0, 0), (0, 0), (1, 1), (0, 0)))
    flat_grad = gradient.reshape(-1, channels)
    stacked = []
    for offset_row in range(3):
        line = []
        for offset_col in range(3):
            window = widened[
                :, offset_row : offset_row + row_count, offset_col : offset_col + col_count, :
            ].reshape(-1, channels)
            line.append(jnp.dot(window.T, flat_grad, preferred_element_type=jnp.float32))
        stacked.append(jnp.stack(line))
    return jnp.stack(stacked)


def body(features, heights, cotangent, weight_first, weight_second, shade_embed):
    images, strip, col_count, channels = features.shape
    space_count = lax.axis_size("space")
    total_rows = strip * space_count
    decline = 2.0 / total_rows
    strip_index = lax.axis_index("space")
    position = (strip_index * strip + jnp.arange(strip)).astype(jnp.float32)
    lifted = heights + decline * position[None, :, None]
    strip_peak = jnp.max(lifted, axis=1)
    carried = prefix(strip_peak, "space", jnp.maximum, jnp.zeros_like(strip_peak))
    running = lax.cummax(lifted, axis=1)
    earlier_max = jnp.concatenate(
        [carried[:, None, :], jnp.maximum(running[:, :-1, :], carried[:, None, :])], axis=1
    )
    shading = jnp.maximum(earlier_max - lifted, 0.0)
    mixed = (
        features.astype(jnp.float32) + shading[..., None] * shade_embed.astype(jnp.float32)
    ).astype(jnp.bfloat16)
    back_second = reversed_kernel(weight_second)
    back_first = reversed_kernel(weight_first)
    padded_in = padded_2(mixed, (("space", 1),), 1)
    hidden_pre = convolve(padded_in, weight_first)
    active = jax.nn.silu(hidden_pre).astype(jnp.bfloat16)
    active_pad = padded_2(active, (("space", 1),), 1)
    cot_pad = padded_2(cotangent, (("space", 1),), 1)
    back_act = convolve(cot_pad, back_second)
    back_hidden = (back_act * silu_slope(hidden_pre)).astype(jnp.bfloat16)
    hidden_pad = padded_2(back_hidden, (("space", 1),), 1)
    back_input = convolve(hidden_pad, back_first)
    grad_features = (cotangent.astype(jnp.float32) + back_input).astype(jnp.bfloat16)
    scaling = 1.0 / math.sqrt(images * lax.axis_size("dp") * total_rows * col_count)
    first_term = kernel_grad(padded_in, back_hidden).reshape(-1) * scaling
    second_term = kernel_grad(active_pad, cotangent).reshape(-1) * scaling
    embed_term = jnp.sum(shading[..., None] * back_input, axis=(0, 1, 2)) * scaling
    first_sum, second_sum, embed_sum = lax.psum(
        (first_term, second_term, embed_term), ("dp", "space")
    )
    kernel_shape = (3, 3, channels, channels)
    return (
        grad_features,
        first_sum.reshape(kernel_shape),
        second_sum.reshape(kernel_shape),
        embed_sum,
    )


def solution(mesh):
    in_specs = (
        P("dp", "space", None, None),
        P("dp", "space", None),
        P("dp", "space", None, None),
        P(),
        P(),
        P(),
    )
    out_specs = (P("dp", "space", None, None), P(), P(), P())
    return jax.shard_map(body, mesh=mesh, in_specs=in_specs, out_specs=out_specs, check_vma=False)
```

profile of v0, /device:TPU:0, one launch (start us, length us, event | category | flops | bytes accessed | tf_op | source)
XLA Modules:
  0.0 250.0 jit_solution(15768503703791382896)
XLA Ops:
  8.8 13.4 %all-gather.1 = f32[8,1,128]{2,1,0:T(1,128)S(1)} all-gather(f32[1,1,128]{2,1,0:T(1,128)S(1)} %bitcast.222), channel_id=2, replica_groups=mesh['dp'=4,'space'=8] {'space'}, dimensions={0}, use_global_device_ids=true | all-gather | bytes 4608 | tf_op jit(solution)/shard_map/all_gather | solution.py:10
  22.1 1.7 copy.38
  24.3 2.2 collective-permute-start.2
  28.5 3.6 %collective-permute-start = (bf16[1,1,128,256]{3,2,1,0:T(8,128)(2,1)}, bf16[1,1,128,256]{3,2,1,0:T(8,128)(2,1)}, u32[]{:S(2)}, u32[]{:S(2)}) collective-permute-start(bf16[1,1,128,256]{3,2,1,0:T(8,128)(2,1)} %get-tuple-element.60), channel_id=1, source_target_pairs={{0,1},{1,2},{2,3},{3,4},{4,5},{5,6},{6,7},{8,9},{9,10},{10,11},{11... | collective-permute-start | bytes 196616 | tf_op jit(solution)/shard_map/ppermute | solution.py:27
  36.1 1.7 pad.11.clone
  39.3 1.8 copy.41
  41.2 4.4 %multiply_convert_fusion.1 = (bf16[16,8,17,256]{3,1,2,0:T(8,128)(2,1)S(1)}, f32[16,8,17,256]{3,1,2,0:T(8,128)}) fusion(pred[8,17]{0,1:T(8,128)(4,1)S(1)} %copy-done.27, bf16[3,3,256,256]{3,2,1,0:T(8,128)(2,1)S(1)} %copy-done, bf16[18,1,7,2,256]{4,2,3,0,1:T(8,128)(2,1)S(1)} %slice.130, bf16[18,1,8,17,256]{4,2,3,0,1:T(8,128)(2,1)S(1)} %copy.41), kind=kOutput, calls=%fused_computation.22 | convolution fusion | flops 2574458880 | bytes 5904520 | tf_op jit(solution)/shard_map/conv_general_dilated | solution.py:37
  50.5 1.9 copy.37
  52.4 4.7 %multiply_convert_fusion = bf16[16,8,17,256]{3,1,2,0:T(8,128)(2,1)S(1)} fusion(f32[16,8,17,256]{3,1,2,0:T(8,128)} %get-tuple-element.65, bf16[3,3,256,256]{3,2,1,0:T(8,128)(2,1)S(1)} %copy-done.26, bf16[18,1,7,2,256]{4,2,3,0,1:T(8,128)(2,1)S(1)} %slice.126, bf16[18,1,8,17,256]{4,2,3,0,1:T(8,128)(2,1)S(1)} %copy.37, pred[8,17]{0,1:T(8,128)(4,1)S(1)} %copy-done.27), kind=kOutput, calls=%fused_computation.21 | convolution fusion | flops 2577244160 | bytes 5904520 | tf_op jit(solution)/shard_map/conv_general_dilated | solution.py:37
  70.5 1.9 copy.60
  73.3 3.8 %collective-permute-start.6 = (bf16[1,1,128,256]{2,3,1,0:T(8,128)(2,1)}, bf16[1,1,128,256]{2,3,1,0:T(8,128)(2,1)}, u32[]{:S(2)}, u32[]{:S(2)}) collective-permute-start(bf16[1,1,128,256]{2,3,1,0:T(8,128)(2,1)} %copy.59), channel_id=1, source_target_pairs={{0,1},{1,2},{2,3},{3,4},{4,5},{5,6},{6,7},{8,9},{9,10},{10,11},{11... | collective-permute-start | bytes 196616 | tf_op jit(solution)/shard_map/ppermute | solution.py:27
  81.6 1.6 maximum_multiply_fusion
  83.2 2.3 fusion.8
  90.4 1.6 maximum_multiply_fusion.1
  93.8 3.7 %collective-permute-start.4 = (bf16[1,1,128,256]{3,2,1,0:T(8,128)(2,1)}, bf16[1,1,128,256]{3,2,1,0:T(8,128)(2,1)S(1)}, u32[]{:S(2)}, u32[]{:S(2)}) collective-permute-start(bf16[1,1,128,256]{3,2,1,0:T(8,128)(2,1)} %slice.132), channel_id=1, source_target_pairs={{0,1},{1,2},{2,3},{3,4},{4,5},{5,6},{6,7},{8,9},{9,10},{10,11},{11... | collective-permute-start | bytes 196616 | tf_op jit(solution)/shard_map/ppermute | solution.py:27
  102.9 1.7 pad.13
  104.5 2.3 reshape.188
  107.2 3.0 %convolution_select_fusion = f32[16,8,17,256]{3,1,2,0:T(8,128)S(1)} fusion(bf16[3,3,256,256]{3,2,1,0:T(8,128)(2,1)S(1)} %copy-done, bf16[18,1,7,2,256]{4,2,3,0,1:T(8,128)(2,1)S(1)} %slice.136, bf16[18,1,8,17,256]{4,2,3,0,1:T(8,128)(2,1)S(1)} %copy.47, pred[8,17]{0,1:T(8,128)(4,1)S(1)} %copy-done.27), kind=kOutput, calls=%fused_computation.29 | convolution fusion | flops 2571673600 | bytes 4790408 | tf_op jit(solution)/shard_map/conv_general_dilated | solution.py:37
  112.5 2.0 copy.58
  114.6 2.7 %fusion.9 = (f32[256]{0:T(256)S(1)}, bf16[1,16,128,256]{2,3,1,0:T(8,128)(2,1)}) fusion(f32[16,1,128,256]{2,3,0,1:T(8,128)S(1)} %copy.58, f32[16,128]{1,0:T(8,128)S(1)} %copy-done.21, bf16[1,16,128,256]{2,3,1,0:T(8,128)(2,1)} %copy.35), kind=kLoop, calls=%fused_computation.26 | loop fusion | flops 2621184 | bytes 4203520 | tf_op jit(solution)/shard_map/reduce_sum | solution.py:107
  117.2 2.3 copy.56
  119.5 42.8 %psum.23 = f32[256]{0:T(256)} all-reduce(f32[256]{0:T(256)S(1)} %broadcast_multiply_fusion), channel_id=1, replica_groups=mesh['dp'=4,'space'=8] {'dp','space'}, use_global_device_ids=true, to_apply=%region_7.8 | all-reduce | flops 256 | bytes 2048 | tf_op jit(solution)/shard_map/psum | solution.py:108
  162.3 76.1 %all-reduce.5.cloned.1.call-done = (f32[3,3,256,256]{3,2,1,0:T(8,128)}, f32[3,3,256,256]{3,2,1,0:T(8,128)}) async-done(((f32[3,3,256,256]{3,2,1,0:T(8,128)}, f32[3,3,256,256]{3,2,1,0:T(8,128)}), (f32[3,3,256,256]{3,2,1,0:T(8,128)}, f32[3,3,256,256]{3,2,1,0:T(8,128)})) %all-reduce.5.cloned.1.call-update) | async-done | bytes 4718608 | tf_op jit(solution)/shard_map/psum | solution.py:108
  238.4 3.4 %copy.109 = f32[3,3,256,256]{3,2,1,0:T(8,128)} copy(f32[3,3,256,256]{3,2,1,0:T(8,128)} %get-tuple-element.118) | data formatting | bytes 4718592
  (140 shorter events, 48.8 us)
Async XLA Ops:
  7.2 34.0 %copy-start = (bf16[3,3,256,256]{3,2,1,0:T(8,128)(2,1)S(1)}, bf16[3,3,256,256]{3,2,1,0:T(8,128)(2,1)}, u32[]{:S(2)}) copy-start(bf16[3,3,256,256]{3,2,1,0:T(8,128)(2,1)} %param.11) | copy-start | bytes 3538948
  7.2 231.2 %all-reduce.5.cloned.1.call-start = ((), (), s32[]{:S(2)}) async-start(), calls=%async_computation | async-start | bytes 9437184 | tf_op jit(solution)/shard_map/psum | solution.py:108
  22.1 5.7 %copy-start.1 = (bf16[1,16,128,256]{3,2,1,0:T(8,128)(2,1)S(1)}, bf16[1,16,128,256]{3,2,1,0:T(8,128)(2,1)}, u32[]{:S(2)}) copy-start(bf16[1,16,128,256]{3,2,1,0:T(8,128)(2,1)} %param.10) | copy-start | bytes 3145732
  23.9 9.6 %copy-start.20 = (f32[16,128]{1,0:T(8,128)}, f32[16,128]{1,0:T(8,128)S(1)}, u32[]{:S(2)}) copy-start(f32[16,128]{1,0:T(8,128)S(1)} %fusion.78) | copy-start | bytes 24580
  24.3 9.2 %copy-start.2 = (bf16[1,16,128,256]{2,3,1,0:T(8,128)(2,1)}, bf16[1,16,128,256]{2,3,1,0:T(8,128)(2,1)S(1)}, u32[]{:S(2)}) copy-start(bf16[1,16,128,256]{2,3,1,0:T(8,128)(2,1)S(1)} %add_convert_fusion) | copy-start | bytes 3145732
  24.3 9.1 %collective-permute-start.2 = (bf16[1,1,128,256]{2,3,1,0:T(8,128)(2,1)S(1)}, bf16[1,1,128,256]{2,3,1,0:T(8,128)(2,1)S(1)}, u32[]{:S(2)}, u32[]{:S(2)}) collective-permute-start(bf16[1,1,128,256]{2,3,1,0:T(8,128)(2,1)S(1)} %get-tuple-element.62), channel_id=1, source_target_pairs={{0,1},{1,2},{2,3},{3,4},{4,5},{5,6},{6,7},{8,9},{9,10},{10,11},{11... | collective-permute-start | bytes 196616 | tf_op jit(solution)/shard_map/ppermute | solution.py:27
  26.6 6.9 %collective-permute-start.3 = (bf16[1,1,128,256]{2,3,1,0:T(8,128)(2,1)S(1)}, bf16[1,1,128,256]{2,3,1,0:T(8,128)(2,1)S(1)}, u32[]{:S(2)}, u32[]{:S(2)}) collective-permute-start(bf16[1,1,128,256]{2,3,1,0:T(8,128)(2,1)S(1)} %get-tuple-element.63), channel_id=1, source_target_pairs={{1,0},{2,1},{3,2},{4,3},{5,4},{6,5},{7,6},{9,8},{10,9},{11,10},{12... | collective-permute-start | bytes 196616 | tf_op jit(solution)/shard_map/ppermute | solution.py:29
  28.5 18.9 %collective-permute-start = (bf16[1,1,128,256]{3,2,1,0:T(8,128)(2,1)}, bf16[1,1,128,256]{3,2,1,0:T(8,128)(2,1)}, u32[]{:S(2)}, u32[]{:S(2)}) collective-permute-start(bf16[1,1,128,256]{3,2,1,0:T(8,128)(2,1)} %get-tuple-element.60), channel_id=1, source_target_pairs={{0,1},{1,2},{2,3},{3,4},{4,5},{5,6},{6,7},{8,9},{9,10},{10,11},{11... | collective-permute-start | bytes 196616 | tf_op jit(solution)/shard_map/ppermute | solution.py:27
  32.2 15.3 %collective-permute-start.1 = (bf16[1,1,128,256]{3,2,1,0:T(8,128)(2,1)}, bf16[1,1,128,256]{3,2,1,0:T(8,128)(2,1)}, u32[]{:S(2)}, u32[]{:S(2)}) collective-permute-start(bf16[1,1,128,256]{3,2,1,0:T(8,128)(2,1)} %get-tuple-element.61), channel_id=1, source_target_pairs={{1,0},{2,1},{3,2},{4,3},{5,4},{6,5},{7,6},{9,8},{10,9},{11,10},{12... | collective-permute-start | bytes 196616 | tf_op jit(solution)/shard_map/ppermute | solution.py:29
  50.5 1.9 copy-start.26
  57.1 3.1 %copy-start.10 = (bf16[16,8,17,256]{3,1,2,0:T(8,128)(2,1)}, bf16[16,8,17,256]{3,1,2,0:T(8,128)(2,1)S(1)}, u32[]{:S(2)}) copy-start(bf16[16,8,17,256]{3,1,2,0:T(8,128)(2,1)S(1)} %multiply_convert_fusion) | copy-start | bytes 3342340
  57.4 2.9 %copy-start.11 = (bf16[1,18,128,256]{2,3,1,0:T(8,128)(2,1)S(1)}, bf16[1,18,128,256]{2,3,1,0:T(8,128)(2,1)}, u32[]{:S(2)}) copy-start(bf16[1,18,128,256]{2,3,1,0:T(8,128)(2,1)} %get-tuple-element.54) | copy-start | bytes 3538948
  58.8 9.2 %copy-start.6 = (bf16[16,1,128,256]{3,0,2,1:T(8,128)(2,1)}, bf16[16,1,128,256]{3,0,2,1:T(8,128)(2,1)S(1)}, u32[]{:S(2)}) copy-start(bf16[16,1,128,256]{3,0,2,1:T(8,128)(2,1)S(1)} %slice.133) | copy-start | bytes 3145732
  69.5 3.0 %copy-start.12 = (bf16[1,8,17,256]{3,1,2,0:T(8,128)(2,1)S(1)}, bf16[1,8,17,256]{3,1,2,0:T(8,128)(2,1)}, u32[]{:S(2)}) copy-start(bf16[1,8,17,256]{3,1,2,0:T(8,128)(2,1)} %get-tuple-element.56) | copy-start | bytes 208900
  73.3 9.9 %collective-permute-start.6 = (bf16[1,1,128,256]{2,3,1,0:T(8,128)(2,1)}, bf16[1,1,128,256]{2,3,1,0:T(8,128)(2,1)}, u32[]{:S(2)}, u32[]{:S(2)}) collective-permute-start(bf16[1,1,128,256]{2,3,1,0:T(8,128)(2,1)} %copy.59), channel_id=1, source_target_pairs={{0,1},{1,2},{2,3},{3,4},{4,5},{5,6},{6,7},{8,9},{9,10},{10,11},{11... | collective-permute-start | bytes 196616 | tf_op jit(solution)/shard_map/ppermute | solution.py:27
  77.1 2.1 copy-start.25
  77.3 1.9 copy-start.4
  77.3 1.9 copy-start.7
  77.3 5.9 %collective-permute-start.7 = (bf16[1,1,128,256]{2,3,1,0:T(8,128)(2,1)S(1)}, bf16[1,1,128,256]{2,3,1,0:T(8,128)(2,1)S(1)}, u32[]{:S(2)}, u32[]{:S(2)}) collective-permute-start(bf16[1,1,128,256]{2,3,1,0:T(8,128)(2,1)S(1)} %copy.61), channel_id=1, source_target_pairs={{1,0},{2,1},{3,2},{4,3},{5,4},{6,5},{7,6},{9,8},{10,9},{11,10},{12... | collective-permute-start | bytes 196616 | tf_op jit(solution)/shard_map/ppermute | solution.py:29
  92.0 8.7 %copy-start.8 = (bf16[16,1,128,256]{3,0,2,1:T(8,128)(2,1)S(1)}, bf16[16,1,128,256]{3,0,2,1:T(8,128)(2,1)}, u32[]{:S(2)}) copy-start(bf16[16,1,128,256]{3,0,2,1:T(8,128)(2,1)} %copy-done.6) | copy-start | bytes 3145732
  93.8 7.4 %collective-permute-start.4 = (bf16[1,1,128,256]{3,2,1,0:T(8,128)(2,1)}, bf16[1,1,128,256]{3,2,1,0:T(8,128)(2,1)S(1)}, u32[]{:S(2)}, u32[]{:S(2)}) collective-permute-start(bf16[1,1,128,256]{3,2,1,0:T(8,128)(2,1)} %slice.132), channel_id=1, source_target_pairs={{0,1},{1,2},{2,3},{3,4},{4,5},{5,6},{6,7},{8,9},{9,10},{10,11},{11... | collective-permute-start | bytes 196616 | tf_op jit(solution)/shard_map/ppermute | solution.py:27
  98.1 4.6 %collective-permute-start.5 = (bf16[1,1,128,256]{3,2,1,0:T(8,128)(2,1)}, bf16[1,1,128,256]{3,2,1,0:T(8,128)(2,1)S(1)}, u32[]{:S(2)}, u32[]{:S(2)}) collective-permute-start(bf16[1,1,128,256]{3,2,1,0:T(8,128)(2,1)} %slice.135), channel_id=1, source_target_pairs={{1,0},{2,1},{3,2},{4,3},{5,4},{6,5},{7,6},{9,8},{10,9},{11,10},{12... | collective-permute-start | bytes 196616 | tf_op jit(solution)/shard_map/ppermute | solution.py:29
  112.5 2.0 copy-start.21
  238.4 3.4 %copy-start.9 = (f32[3,3,256,256]{3,2,1,0:T(8,128)S(1)}, f32[3,3,256,256]{3,2,1,0:T(8,128)}, u32[]{:S(2)}) copy-start(f32[3,3,256,256]{3,2,1,0:T(8,128)} %get-tuple-element.119) | copy-start | bytes 7077892
  (13 other events, 16.1 us)
Sparse Core Ops, SparseCore 0:
  92.2 146.1 all-reduce.4
where the time goes:
time: 251 us; the launch traced here: 250 us
  waiting for transfers between devices  77.7 us (31%)
  blocking collectives  56.1 us (22%)
  local copies, waits for them, and re-layouts  40.5 us (16%)
  matrix products  29.5 us (12%)
  starting transfers between devices  18.6 us (7%)
  between operations  14.7 us (6%)
  other arithmetic  12.8 us (5%)
    psum x1, waiting for transfers between devices, body(): lax.psum((first_term, second_term, embed_term), ('dp', 'space'))  76.1 us
    psum x1, blocking collectives, body(): lax.psum((first_term, second_term, embed_term), ('dp', 'space'))  42.8 us
    unnamed x67, local copies, waits for them, and re-layouts  18.6 us
    dot_general x18, matrix products, kernel_grad(): jnp.dot(window.T, flat_grad, preferred_element_type=jnp.float32)  17.4 us
    all_gather x1, blocking collectives, prefix(): gathered = lax.all_gather(part, axis)  13.4 us
    ppermute x4, starting transfers between devices, padded_2(): lax.ppermute(tail, axis, [(i, (i + 1) % count) for i in range(ends)])  13.3 us
    conv_general_dilated x3, matrix products, convolve(): lax.conv_general_dilated(padded, kernel, (1, 1), ((0, 0), (1, 1)), dimens...  12.1 us
    conv_general_dilated x11, local copies, waits for them, and re-layouts, convolve(): lax.conv_general_dilated(padded, kernel, (1, 1), ((0, 0), (1, 1)), dimens...  11.5 us
  transfers between devices with their start and end apart: 9, of which 2 were waited for; matrix products, arithmetic and copies ran while one was open for 16% of the time, Pallas kernels for 0%

commit v1 on v0

--- a/solution.py
+++ b/solution.py
@@ -106,7 +106,7 @@
     second_term = kernel_grad(active_pad, cotangent).reshape(-1) * scaling
     embed_term = jnp.sum(shading[..., None] * back_input, axis=(0, 1, 2)) * scaling
     first_sum, second_sum, embed_sum = lax.psum(
-        (first_term, second_term, embed_term), ("dp", "space")
+        lax.psum((first_term, second_term, embed_term), "space"), "dp"
     )
     kernel_shape = (3, 3, channels, channels)
     return (

time: 251 us -> 335 us (1.33)
  waiting for transfers between devices: 77.7 us -> 169 us
  blocking collectives: 56.1 us -> 40.9 us
  local copies, waits for them, and re-layouts: 40.5 us -> 53 us
    psum x1 -> x2, waiting for transfers between devices: 76.1 us -> 168 us  [the longest x1 108 us: body(): lax.psum((first_term, second_term, embed_term), 'space')]
    psum x1 -> x2, blocking collectives: 42.8 us -> 27.5 us  [the longest x1 16.8 us: body(): lax.psum((first_term, second_term, embed_term), 'space')]
    reshape x0 -> x2, local copies, waits for them, and re-layouts: none -> 6.96 us  [the longest x1 3.48 us: body(): first_sum.reshape(kernel_shape)]
    unnamed x67 -> x69, local copies, waits for them, and re-layouts: 18.6 us -> 24.2 us
  transfers between devices with their start and end apart: 9 -> 10, of which waited for: 2 -> 3; matrix products, arithmetic and copies ran while one was open for 16% -> 12% of each run, Pallas kernels for 0% -> 0%
where the time goes in v1:
time: 335 us; the launch traced here: 334 us
  waiting for transfers between devices  169 us (50%)
  local copies, waits for them, and re-layouts  53 us (16%)
  blocking collectives  40.9 us (12%)
  matrix products  29.5 us (9%)
  starting transfers between devices  16.7 us (5%)
  between operations  14.7 us (4%)
  other arithmetic  9.97 us (3%)
    psum x1, waiting for transfers between devices, body(): lax.psum((first_term, second_term, embed_term), 'space')  108 us
    psum x1, waiting for transfers between devices, body(): lax.psum(lax.psum((first_term, second_term, embed_term), 'space'), 'dp')  60.1 us
    unnamed x69, local copies, waits for them, and re-layouts  24.2 us
    dot_general x18, matrix products, kernel_grad(): jnp.dot(window.T, flat_grad, preferred_element_type=jnp.float32)  17.4 us
    psum x1, blocking collectives, body(): lax.psum((first_term, second_term, embed_term), 'space')  16.8 us
    all_gather x1, blocking collectives, prefix(): gathered = lax.all_gather(part, axis)  13.4 us
    conv_general_dilated x3, matrix products, convolve(): lax.conv_general_dilated(padded, kernel, (1, 1), ((0, 0), (1, 1)), dimens...  12.1 us
    conv_general_dilated x11, local copies, waits for them, and re-layouts, convolve(): lax.conv_general_dilated(padded, kernel, (1, 1), ((0, 0), (1, 1)), dimens...  11.6 us
  transfers between devices with their start and end apart: 10, of which 3 were waited for; matrix products, arithmetic and copies ran while one was open for 12% of the time, Pallas kernels for 0%

profile of v1, /device:TPU:0, one launch (start us, length us, event | category | flops | bytes accessed | tf_op | source)
XLA Modules:
  0.0 334.3 jit_solution(11482023445694179087)
XLA Ops:
  8.8 13.4 %all-gather.1 = f32[8,1,128]{2,1,0:T(1,128)S(1)} all-gather(f32[1,1,128]{2,1,0:T(1,128)S(1)} %bitcast.230), channel_id=2, replica_groups=mesh['dp'=4,'space'=8] {'space'}, dimensions={0}, use_global_device_ids=true | all-gather | bytes 4608 | tf_op jit(solution)/shard_map/all_gather | solution.py:10
  24.3 2.2 collective-permute-start.2
  28.5 3.6 %collective-permute-start = (bf16[1,1,128,256]{3,2,1,0:T(8,128)(2,1)}, bf16[1,1,128,256]{3,2,1,0:T(8,128)(2,1)}, u32[]{:S(2)}, u32[]{:S(2)}) collective-permute-start(bf16[1,1,128,256]{3,2,1,0:T(8,128)(2,1)} %get-tuple-element.62), channel_id=1, source_target_pairs={{0,1},{1,2},{2,3},{3,4},{4,5},{5,6},{6,7},{8,9},{9,10},{10,11},{11... | collective-permute-start | bytes 196616 | tf_op jit(solution)/shard_map/ppermute | solution.py:27
  39.3 1.8 copy.41
  41.2 4.4 %multiply_convert_fusion.1 = (bf16[16,8,17,256]{3,1,2,0:T(8,128)(2,1)S(1)}, f32[16,8,17,256]{3,1,2,0:T(8,128)}) fusion(pred[8,17]{0,1:T(8,128)(4,1)S(1)} %copy-done.27, bf16[3,3,256,256]{3,2,1,0:T(8,128)(2,1)S(1)} %copy-done, bf16[18,1,7,2,256]{4,2,3,0,1:T(8,128)(2,1)S(1)} %slice.130, bf16[18,1,8,17,256]{4,2,3,0,1:T(8,128)(2,1)S(1)} %copy.41), kind=kOutput, calls=%fused_computation.22 | convolution fusion | flops 2574458880 | bytes 5904520 | tf_op jit(solution)/shard_map/conv_general_dilated | solution.py:37
  50.4 1.9 copy.37
  52.4 4.7 %multiply_convert_fusion = bf16[16,8,17,256]{3,1,2,0:T(8,128)(2,1)S(1)} fusion(f32[16,8,17,256]{3,1,2,0:T(8,128)} %get-tuple-element.67, bf16[3,3,256,256]{3,2,1,0:T(8,128)(2,1)S(1)} %copy-done.26, bf16[18,1,7,2,256]{4,2,3,0,1:T(8,128)(2,1)S(1)} %slice.126, bf16[18,1,8,17,256]{4,2,3,0,1:T(8,128)(2,1)S(1)} %copy.37, pred[8,17]{0,1:T(8,128)(4,1)S(1)} %copy-done.27), kind=kOutput, calls=%fused_computation.21 | convolution fusion | flops 2577244160 | bytes 5904520 | tf_op jit(solution)/shard_map/conv_general_dilated | solution.py:37
  70.5 1.9 copy.60
  73.3 3.8 %collective-permute-start.6 = (bf16[1,1,128,256]{2,3,1,0:T(8,128)(2,1)}, bf16[1,1,128,256]{2,3,1,0:T(8,128)(2,1)}, u32[]{:S(2)}, u32[]{:S(2)}) collective-permute-start(bf16[1,1,128,256]{2,3,1,0:T(8,128)(2,1)} %copy.59), channel_id=1, source_target_pairs={{0,1},{1,2},{2,3},{3,4},{4,5},{5,6},{6,7},{8,9},{9,10},{10,11},{11... | collective-permute-start | bytes 196616 | tf_op jit(solution)/shard_map/ppermute | solution.py:27
  81.8 2.6 copy.63
  84.5 2.3 fusion.8
  91.8 2.6 copy.64
  94.5 107.9 %all-reduce.7.cloned.1.call-done = (f32[589824]{0:T(1024)}, f32[589824]{0:T(1024)}) async-done(((f32[589824]{0:T(1024)}, f32[589824]{0:T(1024)}), (f32[589824]{0:T(1024)}, f32[589824]{0:T(1024)})) %all-reduce.7.cloned.1.call-update) | async-done | bytes 4718608 | tf_op jit(solution)/shard_map/psum | solution.py:109
  202.4 3.5 %reshape.150 = f32[3,3,256,256]{3,2,1,0:T(8,128)} reshape(f32[589824]{0:T(1024)} %get-tuple-element.48) | data formatting | bytes 4718592 | tf_op jit(solution)/shard_map/reshape | solution.py:114
  205.9 3.5 %reshape.161 = f32[3,3,256,256]{3,2,1,0:T(8,128)} reshape(f32[589824]{0:T(1024)} %get-tuple-element.49) | data formatting | bytes 4718592 | tf_op jit(solution)/shard_map/reshape | solution.py:115
  220.0 2.3 reshape.186
  222.7 3.0 convolution_select_fusion
  228.0 2.1 copy.58
  230.2 2.6 fusion.9
  232.8 2.3 copy.56
  235.1 16.8 %psum.46 = f32[256]{0:T(256)S(1)} all-reduce(f32[256]{0:T(256)S(1)} %broadcast_multiply_fusion), channel_id=1, replica_groups=mesh['dp'=4,'space'=8] {'space'}, use_global_device_ids=true, to_apply=%region_9.10 | all-reduce | flops 256 | bytes 2048 | tf_op jit(solution)/shard_map/psum | solution.py:109
  251.9 10.7 %psum.47 = f32[256]{0:T(256)} all-reduce(f32[256]{0:T(256)S(1)} %psum.46), channel_id=1, replica_groups=mesh['dp'=4,'space'=8] {'dp'}, use_global_device_ids=true, to_apply=%region_10.11 | all-reduce | flops 256 | bytes 2048 | tf_op jit(solution)/shard_map/psum | solution.py:108
  262.6 60.1 %all-reduce.9.cloned.1.call-done = (f32[3,3,256,256]{3,2,1,0:T(8,128)}, f32[3,3,256,256]{3,2,1,0:T(8,128)}) async-done(((f32[3,3,256,256]{3,2,1,0:T(8,128)}, f32[3,3,256,256]{3,2,1,0:T(8,128)}), (f32[3,3,256,256]{3,2,1,0:T(8,128)}, f32[3,3,256,256]{3,2,1,0:T(8,128)})) %all-reduce.9.cloned.1.call-update) | async-done | bytes 4718608 | tf_op jit(solution)/shard_map/psum | solution.py:108
  322.6 3.4 %copy.113 = f32[3,3,256,256]{3,2,1,0:T(8,128)} copy(f32[3,3,256,256]{3,2,1,0:T(8,128)} %get-tuple-element.120) | data formatting | bytes 4718592
  (148 shorter events, 56.0 us)
Async XLA Ops:
  7.2 34.0 %copy-start = (bf16[3,3,256,256]{3,2,1,0:T(8,128)(2,1)S(1)}, bf16[3,3,256,256]{3,2,1,0:T(8,128)(2,1)}, u32[]{:S(2)}) copy-start(bf16[3,3,256,256]{3,2,1,0:T(8,128)(2,1)} %param.11) | copy-start | bytes 3538948
  7.2 195.3 %all-reduce.7.cloned.1.call-start = ((), (), s32[]{:S(2)}) async-start(), calls=%async_computation | async-start | bytes 9437184 | tf_op jit(solution)/shard_map/psum | solution.py:109
  22.1 5.7 %copy-start.1 = (bf16[1,16,128,256]{3,2,1,0:T(8,128)(2,1)S(1)}, bf16[1,16,128,256]{3,2,1,0:T(8,128)(2,1)}, u32[]{:S(2)}) copy-start(bf16[1,16,128,256]{3,2,1,0:T(8,128)(2,1)} %param.10) | copy-start | bytes 3145732
  23.9 9.6 %copy-start.20 = (f32[16,128]{1,0:T(8,128)}, f32[16,128]{1,0:T(8,128)S(1)}, u32[]{:S(2)}) copy-start(f32[16,128]{1,0:T(8,128)S(1)} %fusion.78) | copy-start | bytes 24580
  24.3 9.2 %copy-start.2 = (bf16[1,16,128,256]{2,3,1,0:T(8,128)(2,1)}, bf16[1,16,128,256]{2,3,1,0:T(8,128)(2,1)S(1)}, u32[]{:S(2)}) copy-start(bf16[1,16,128,256]{2,3,1,0:T(8,128)(2,1)S(1)} %add_convert_fusion) | copy-start | bytes 3145732
  24.3 9.1 %collective-permute-start.2 = (bf16[1,1,128,256]{2,3,1,0:T(8,128)(2,1)S(1)}, bf16[1,1,128,256]{2,3,1,0:T(8,128)(2,1)S(1)}, u32[]{:S(2)}, u32[]{:S(2)}) collective-permute-start(bf16[1,1,128,256]{2,3,1,0:T(8,128)(2,1)S(1)} %get-tuple-element.64), channel_id=1, source_target_pairs={{0,1},{1,2},{2,3},{3,4},{4,5},{5,6},{6,7},{8,9},{9,10},{10,11},{11... | collective-permute-start | bytes 196616 | tf_op jit(solution)/shard_map/ppermute | solution.py:27
  26.6 6.9 %collective-permute-start.3 = (bf16[1,1,128,256]{2,3,1,0:T(8,128)(2,1)S(1)}, bf16[1,1,128,256]{2,3,1,0:T(8,128)(2,1)S(1)}, u32[]{:S(2)}, u32[]{:S(2)}) collective-permute-start(bf16[1,1,128,256]{2,3,1,0:T(8,128)(2,1)S(1)} %get-tuple-element.65), channel_id=1, source_target_pairs={{1,0},{2,1},{3,2},{4,3},{5,4},{6,5},{7,6},{9,8},{10,9},{11,10},{12... | collective-permute-start | bytes 196616 | tf_op jit(solution)/shard_map/ppermute | solution.py:29
  28.5 18.9 %collective-permute-start = (bf16[1,1,128,256]{3,2,1,0:T(8,128)(2,1)}, bf16[1,1,128,256]{3,2,1,0:T(8,128)(2,1)}, u32[]{:S(2)}, u32[]{:S(2)}) collective-permute-start(bf16[1,1,128,256]{3,2,1,0:T(8,128)(2,1)} %get-tuple-element.62), channel_id=1, source_target_pairs={{0,1},{1,2},{2,3},{3,4},{4,5},{5,6},{6,7},{8,9},{9,10},{10,11},{11... | collective-permute-start | bytes 196616 | tf_op jit(solution)/shard_map/ppermute | solution.py:27
  32.2 15.2 %collective-permute-start.1 = (bf16[1,1,128,256]{3,2,1,0:T(8,128)(2,1)}, bf16[1,1,128,256]{3,2,1,0:T(8,128)(2,1)}, u32[]{:S(2)}, u32[]{:S(2)}) collective-permute-start(bf16[1,1,128,256]{3,2,1,0:T(8,128)(2,1)} %get-tuple-element.63), channel_id=1, source_target_pairs={{1,0},{2,1},{3,2},{4,3},{5,4},{6,5},{7,6},{9,8},{10,9},{11,10},{12... | collective-permute-start | bytes 196616 | tf_op jit(solution)/shard_map/ppermute | solution.py:29
  50.4 1.9 copy-start.26
  57.1 3.1 copy-start.10
  57.4 2.9 copy-start.11
  58.7 9.2 %copy-start.6 = (bf16[16,1,128,256]{3,0,2,1:T(8,128)(2,1)}, bf16[16,1,128,256]{3,0,2,1:T(8,128)(2,1)S(1)}, u32[]{:S(2)}) copy-start(bf16[16,1,128,256]{3,0,2,1:T(8,128)(2,1)S(1)} %slice.133) | copy-start | bytes 3145732
  69.5 3.0 copy-start.12
  73.3 11.2 %collective-permute-start.6 = (bf16[1,1,128,256]{2,3,1,0:T(8,128)(2,1)}, bf16[1,1,128,256]{2,3,1,0:T(8,128)(2,1)}, u32[]{:S(2)}, u32[]{:S(2)}) collective-permute-start(bf16[1,1,128,256]{2,3,1,0:T(8,128)(2,1)} %copy.59), channel_id=1, source_target_pairs={{0,1},{1,2},{2,3},{3,4},{4,5},{5,6},{6,7},{8,9},{9,10},{10,11},{11... | collective-permute-start | bytes 196616 | tf_op jit(solution)/shard_map/ppermute | solution.py:27
  77.1 2.1 copy-start.25
  77.3 1.9 copy-start.4
  77.3 7.1 %collective-permute-start.7 = (bf16[1,1,128,256]{2,3,1,0:T(8,128)(2,1)S(1)}, bf16[1,1,128,256]{2,3,1,0:T(8,128)(2,1)S(1)}, u32[]{:S(2)}, u32[]{:S(2)}) collective-permute-start(bf16[1,1,128,256]{2,3,1,0:T(8,128)(2,1)S(1)} %copy.61), channel_id=1, source_target_pairs={{1,0},{2,1},{3,2},{4,3},{5,4},{6,5},{7,6},{9,8},{10,9},{11,10},{12... | collective-permute-start | bytes 196616 | tf_op jit(solution)/shard_map/ppermute | solution.py:29
  94.5 228.2 %all-reduce.9.cloned.1.call-start = ((), (), s32[]{:S(2)}) async-start(), calls=%async_computation.1 | async-start | bytes 9437184 | tf_op jit(solution)/shard_map/psum | solution.py:108
  209.4 7.0 %copy-start.8 = (bf16[16,1,128,256]{3,0,2,1:T(8,128)(2,1)S(1)}, bf16[16,1,128,256]{3,0,2,1:T(8,128)(2,1)}, u32[]{:S(2)}) copy-start(bf16[16,1,128,256]{3,0,2,1:T(8,128)(2,1)} %copy-done.6) | copy-start | bytes 3145732
  211.2 5.6 %collective-permute-start.4 = (bf16[1,1,128,256]{3,2,1,0:T(8,128)(2,1)}, bf16[1,1,128,256]{3,2,1,0:T(8,128)(2,1)S(1)}, u32[]{:S(2)}, u32[]{:S(2)}) collective-permute-start(bf16[1,1,128,256]{3,2,1,0:T(8,128)(2,1)} %slice.132), channel_id=1, source_target_pairs={{0,1},{1,2},{2,3},{3,4},{4,5},{5,6},{6,7},{8,9},{9,10},{10,11},{11... | collective-permute-start | bytes 196616 | tf_op jit(solution)/shard_map/ppermute | solution.py:27
  213.5 4.7 %collective-permute-start.5 = (bf16[1,1,128,256]{3,2,1,0:T(8,128)(2,1)}, bf16[1,1,128,256]{3,2,1,0:T(8,128)(2,1)S(1)}, u32[]{:S(2)}, u32[]{:S(2)}) collective-permute-start(bf16[1,1,128,256]{3,2,1,0:T(8,128)(2,1)} %slice.135), channel_id=1, source_target_pairs={{1,0},{2,1},{3,2},{4,3},{5,4},{6,5},{7,6},{9,8},{10,9},{11,10},{12... | collective-permute-start | bytes 196616 | tf_op jit(solution)/shard_map/ppermute | solution.py:29
  228.0 2.1 copy-start.21
  322.6 3.4 %copy-start.9 = (f32[3,3,256,256]{3,2,1,0:T(8,128)S(1)}, f32[3,3,256,256]{3,2,1,0:T(8,128)}, u32[]{:S(2)}) copy-start(f32[3,3,256,256]{3,2,1,0:T(8,128)} %get-tuple-element.121) | copy-start | bytes 7077892
  (14 other events, 18.0 us)
Sparse Core Ops, SparseCore 0:
  94.6 107.7 all-reduce.6
  209.5 113.0 all-reduce.8
